TPU v7x, 32 devices: a whole 2x2x4 slice. The times are simulated.
32 devices in a mesh: sub: 8 (over z, x), layer: 4 (over y, core).
Axes of the slice: x: 2, y: 2, z: 4, core: 2. Of those that a mesh axis runs over, the one named last changes fastest.
Arguments:
- local_gap: float32 [8, 4, 1152, 128], P('sub', 'layer'), may hold values from -6 to 6
- route_codes: int32 [8, 4, 1152], P('sub', 'layer'), may hold values from 0 to 1152, as said below
- flexibility: float32 [8, 4, 1152, 1152], P('sub', 'layer'), may hold values from -1 to 3
- dirichlet: float32 [8, 4, 1152, 1152], P('sub', 'layer'), may hold values from -1 to 3
- rigid_modes: float32 [8, 4, 6, 1152], P('sub', 'layer'), may hold values from -6 to 6
- coarse_inverse: float32 [192, 192], P(('sub', 'layer')), may hold values from -1 to 1
- rigid_load: float32 [192, 128], P(('sub', 'layer')), may hold values from -360 to 360
Outputs:
- multipliers: float32 [8, 4, 1152, 128], P('sub', 'layer')
- residual: float32 [8, 4, 1152, 128], P('sub', 'layer')
Inputs may be any that keep to these rules, and one draw needn't show every extreme that they name: `route_codes`: row r of subdomain (i, j) carries d * 288 + k when it is the k-th row it shares with neighbour d (0: sub index i - 1, 1: i + 1, 2: layer index j - 1, 3: j + 1); the row of that neighbour carrying e * 288 + k, e the opposite direction, is the same interface row. 4 * 288 marks a row shared with nobody. Neighbouring subdomains share between 144 and 288 rows, some pair exactly 288; there is no neighbour beyond the ends of an axis.
All inputs are finite; a program needn't handle non-finite values.
Results may differ from a plain program's by a relative error of at most 0.00017.
Values sent between devices are 32-bit elements; how exact they have to be, the bound alone decides.
No kernel may reach another device: no remote copies, remote signals or barrier semaphores. Data moves between devices by JAX's collectives and lax.ppermute only.
A program may use at most 128 MiB of HBM per device.

v0:
```python
import functools

import jax
import jax.numpy as jnp
from jax import lax
from jax.experimental import pallas as pl
from jax.experimental.pallas import tpu as pltpu
from jax.sharding import PartitionSpec as P

theta_mid = 4.25
delta_half = 3.75
sigma_ratio = theta_mid / delta_half
damping = delta_half / theta_mid
damping_next = 1.0 / (2.0 * sigma_ratio - damping)
keep_step = damping_next * damping
new_step = 2.0 * damping_next / delta_half

GROUP = 32
PAD = 8
SIDES = 4


def exact(a, b, contract=((1,), (0,))):
    return lax.dot_general(
        a,
        b,
        (contract, ((), ())),
        precision=lax.Precision.HIGHEST,
        preferred_element_type=jnp.float32,
    )


def one_pass(a, b):
    return jnp.dot(a, b, preferred_element_type=jnp.float32)


def two_pieces(x):
    high = x.astype(jnp.bfloat16)
    low = (x - high.astype(jnp.float32)).astype(jnp.bfloat16)
    return high, low


def slot_by_row(codes_row, start, rows):
    slots = lax.broadcasted_iota(jnp.int32, (rows, codes_row.shape[1]), 0) + start
    return jnp.where(slots == codes_row, 1.0, 0.0).astype(jnp.bfloat16)


def row_by_slot(codes_lanes, slots):
    rows, lanes = codes_lanes.shape
    lane = lax.broadcasted_iota(jnp.int32, (rows, lanes), 1)
    parts = [
        jnp.where(lane + first == codes_lanes, 1.0, 0.0).astype(jnp.bfloat16)
        for first in range(0, slots, lanes)
    ]
    return jnp.concatenate(parts, axis=1)


def fill_pieces(pieces, start, x):
    high, low = two_pieces(x)
    cols = x.shape[1]
    pieces[pl.ds(start, x.shape[0]), 0:cols] = high
    pieces[pl.ds(start, x.shape[0]), cols : 2 * cols] = low


def to_rows(codes_lanes, slot_pieces, write):
    total = slot_pieces.shape[0]
    chunk = total // SIDES
    for c in range(SIDES):
        pick = row_by_slot(codes_lanes[c * chunk : (c + 1) * chunk, :], total)
        write(c * chunk, one_pass(pick, slot_pieces[...]))


def halves(x):
    cols = x.shape[1] // 2
    return x[:, :cols] + x[:, cols:]


def fetch(matrix, held, arrived):
    chunk = held.shape[0] // SIDES
    pieces = []
    for c in range(SIDES):
        rows = pl.ds(c * chunk, chunk)
        pieces.append(pltpu.make_async_copy(matrix.at[rows], held.at[rows], arrived.at[c]))
        pieces[c].start()
    return pieces, held


def apply_local(fetched, codes_row, codes_lanes, slot_pieces, row_pieces, out_pieces, write, less=None):
    total = slot_pieces.shape[0]
    chunk = total // SIDES

    def keep(start, rows):
        row_pieces[start : start + chunk, :] = rows.astype(jnp.bfloat16)

    to_rows(codes_lanes, slot_pieces, keep)
    apply_rows(fetched, codes_row, row_pieces, out_pieces, write, less)


def apply_rows(fetched, codes_row, row_pieces, out_pieces, write, less=None):
    coming, matrix = fetched
    total = row_pieces.shape[0]
    chunk = total // SIDES
    cols = row_pieces.shape[1] // 2
    for c in range(SIDES):
        coming[c].wait()
        high, low = two_pieces(matrix[c * chunk : (c + 1) * chunk, :])
        product = halves(one_pass(high, row_pieces[...])) + one_pass(low, row_pieces[:, :cols])
        if less is not None:
            product = less[c * chunk : (c + 1) * chunk, :] - product
        fill_pieces(out_pieces, c * chunk, product)
    for side in range(SIDES):
        pick = slot_by_row(codes_row[...], side * chunk, chunk)
        write(side, halves(one_pass(pick, out_pieces[...])))


def three_pass(a, b):
    a_high, a_low = two_pieces(a)
    b_high, b_low = two_pieces(b)
    both = jnp.concatenate([b_high, b_low], axis=1)
    return halves(one_pass(a_high, both)) + one_pass(a_low, b_high)


def copies(ref, block):
    rows = block.shape[0]
    for q in range(ref.shape[0] // rows):
        ref[q * rows : (q + 1) * rows, :] = block


def modes_kernel(mode_count, codes_row, modes, inverse, load, *outs):
    total = codes_row.shape[1]
    cap = total // SIDES
    codes = codes_row[...]
    heading = codes // cap
    i, j = lax.axis_index("sub"), lax.axis_index("layer")
    even = jnp.where(heading < 2, 1 - lax.rem(i, 2), 1 - lax.rem(j, 2))
    turn = jnp.where(heading < SIDES, even * (1 - 2 * (heading % 2)), 0)
    codes = codes + turn * cap
    outs[SIDES + 3][...] = codes
    codes = jnp.broadcast_to(codes, (128, total)).astype(jnp.float32)
    codes_lanes = jnp.transpose(codes).astype(jnp.int32)
    x = jnp.concatenate(
        [modes[:, 0, :], jnp.zeros((PAD - mode_count, total), jnp.float32)], axis=0
    )
    high = x.astype(jnp.bfloat16).astype(jnp.float32)
    middle = (x - high).astype(jnp.bfloat16).astype(jnp.float32)
    low = x - high - middle
    pieces = jnp.concatenate([high, middle, low, jnp.zeros_like(low)], axis=0).astype(jnp.bfloat16)
    moved = one_pass(pieces, row_by_slot(codes_lanes, total))
    upper, lower = moved[0:PAD], moved[PAD : 2 * PAD]
    moved = upper + lower + moved[2 * PAD : 3 * PAD]
    for side in range(SIDES):
        outs[side][...] = moved[:, side * cap : (side + 1) * cap]
    coarse = inverse.shape[1]
    padded = coarse // mode_count * PAD
    old = lax.broadcasted_iota(jnp.int32, (coarse, padded), 0)
    new = lax.broadcasted_iota(jnp.int32, (coarse, padded), 1)
    spread = jnp.where((old // mode_count) * PAD + old % mode_count == new, 1.0, 0.0)
    blank = jnp.zeros((PAD - mode_count, coarse), jnp.float32)
    wide = exact(jnp.concatenate([inverse[...], blank], axis=0), spread)
    blank = jnp.zeros((PAD - mode_count, load.shape[1]), jnp.float32)
    loads = jnp.concatenate([load[...], blank], axis=0)
    copies(outs[SIDES], jnp.concatenate([wide, loads], axis=1))
    outs[SIDES + 1][...] = codes_lanes
    outs[SIDES + 2][...] = jnp.concatenate([upper, lower], axis=0)


def around(i, j):
    right, up = 1 - 2 * (i % 2), 1 - 2 * (j % 2)
    return [(i, j), (i + right, j), (i - right, j), (i, j + up), (i, j - up)]


def mode_blocks(own, partner):
    cap = own[0].shape[1]
    rows = []
    for side in range(SIDES):
        column = [own[side][...]]
        for other in range(SIDES):
            if other == side:
                column.append(-partner[side][...])
            else:
                column.append(jnp.zeros((PAD, cap), jnp.float32))
        rows.append(jnp.concatenate(column, axis=0))
    return rows


def lane_spread(mode_count, lanes):
    shape = (PAD * (SIDES + 1), lanes)
    old = lax.broadcasted_iota(jnp.int32, shape, 0)
    new = lax.broadcasted_iota(jnp.int32, shape, 1)
    spot = (old // PAD) * mode_count + old % PAD
    match = (spot == new % GROUP) & (old % PAD < mode_count)
    return jnp.where(match, 1.0, 0.0)


def operators_kernel(mode_count, flex, schur, codes_row, codes_lanes, *refs):
    own, partner = refs[0:4], refs[4:8]
    outs = refs[8:12]
    modes_out = refs[12]
    slot_pieces, row_pieces, out_pieces = refs[13:16]
    schur = fetch(schur, refs[16], refs[17])
    flex = fetch(flex, refs[18], refs[19])
    total = codes_lanes.shape[0]
    cap = total // SIDES
    half = cap // 2
    lanes = 4 * GROUP
    spread = lane_spread(mode_count, lanes)
    for side, block in enumerate(mode_blocks(own, partner)):
        placed = exact(block, spread, ((0,), (0,)))
        first = lax.broadcasted_iota(jnp.int32, placed.shape, 1) < GROUP
        modes_out[side * cap : (side + 1) * cap, :] = jnp.where(first, placed, 0.0)
        fill_pieces(slot_pieces, side * cap, placed)
    group = lax.broadcasted_iota(jnp.int32, (half, lanes), 1) // GROUP

    def write_schur(side, block):
        outs[side][...] = jnp.where(group == 0, block[:half], block[half:])

    def write_flex(side, block):
        mine = jnp.where(group == 2, block[:half], block[half:])
        outs[side][...] = jnp.where(group < 2, outs[side][...], mine)

    apply_local(schur, codes_row, codes_lanes, slot_pieces, row_pieces, out_pieces, write_schur)
    apply_rows(flex, codes_row, row_pieces, out_pieces, write_flex)


def start_kernel(mode_count, layers, flex, gap, codes_row, codes_lanes, *refs):
    slabs = refs[0:4]
    gathered, modes = refs[4:6]
    outs = refs[6:10]
    start_out, inverse_out = refs[10:12]
    slot_pieces, row_pieces, out_pieces = refs[12:15]
    flex = fetch(flex, refs[15], refs[16])
    cap = codes_lanes.shape[0] // SIDES
    wide = gathered.shape[0]
    spread = lane_spread(mode_count, GROUP)
    for n, centre in enumerate(around(lax.axis_index("sub"), lax.axis_index("layer"))):
        rows = []
        for i, j in around(*centre):
            first = jnp.clip(i * layers + j, 0, wide // PAD - 1) * PAD
            rows.append(gathered[pl.ds(pl.multiple_of(first, PAD), PAD), 0:wide])
        table = jnp.concatenate(rows, axis=0)
        inverse_out[n * GROUP : (n + 1) * GROUP, :] = exact(spread, table, ((0,), (0,)))
    coefficients = repeated(exact(inverse_out[0:GROUP, :], gathered[:, wide:]))
    start = three_pass(modes[...], coefficients)
    start_out[...] = start
    fill_pieces(slot_pieces, 0, start)

    def write(side, block):
        outs[side][0:cap, :] = block
        outs[side][cap:, :] = slabs[side][...]

    apply_local(flex, codes_row, codes_lanes, slot_pieces, row_pieces, out_pieces, write, gap)


def repeated(x):
    return jnp.concatenate([x] * 4, axis=0)


def components_of(own_pieces, block_pieces):
    both = one_pass(own_pieces[...].astype(jnp.bfloat16), block_pieces[...])
    cols = both.shape[1] // 2
    return halves(both[0:PAD]) + both[PAD:, :cols]


def grouped(slab, first):
    group = lax.broadcasted_iota(jnp.int32, slab.shape, 1) // GROUP
    upper = jnp.where(group == first, slab, 0.0)
    lower = jnp.where(group == first + 1, slab, 0.0)
    return jnp.concatenate([upper, lower], axis=0)


def lagged(side, first, mine, theirs, coefficients):
    left = jnp.concatenate([grouped(mine, first), grouped(theirs, first)], axis=1)
    near = coefficients[(side + 1) * GROUP : (side + 2) * GROUP]
    return three_pass(left, jnp.concatenate([repeated(coefficients[0:GROUP]), repeated(-near)], axis=0))


def first_kernel(schur, codes_row, codes_lanes, *refs):
    received, sent, own = refs[0:4], refs[4:8], refs[8]
    outs = refs[9:13]
    gap_out, parts_out, mine_out, theirs_out = refs[13:17]
    slot_pieces, row_pieces, out_pieces = refs[17:20]
    schur = fetch(schur, refs[20], refs[21])
    half = sent[0].shape[0] - codes_lanes.shape[0] // SIDES
    cap = codes_lanes.shape[0] // SIDES
    for side in range(SIDES):
        block = sent[side][0:cap, :] - received[side][0:cap, :]
        gap_out[side * cap : (side + 1) * cap, :] = block
        fill_pieces(slot_pieces, side * cap, block)
        mine_out[side * half : (side + 1) * half, :] = sent[side][cap:, :]
        theirs_out[side * half : (side + 1) * half, :] = received[side][cap:, :]
    copies(parts_out, components_of(own, slot_pieces))

    def write(side, block):
        outs[side][...] = block

    apply_local(schur, codes_row, codes_lanes, slot_pieces, row_pieces, out_pieces, write)


def stage_kernel(stage, matrix, codes_row, codes_lanes, *refs):
    refs = list(refs)

    def take(count):
        taken = refs[:count]
        del refs[:count]
        return taken

    received, sent = take(4), take(4)
    mine, theirs, own, gathered, inverse_rows = take(5)
    (state_in,) = take(1) if stage > 2 else [None]
    outs = take(4) if stage < 5 else []
    state_out, parts_out = take(2)
    slot_pieces, row_pieces, out_pieces = take(3)
    if stage < 5:
        matrix = fetch(matrix, *take(2))
    total = codes_lanes.shape[0]
    cap = total // SIDES
    half = mine.shape[0] // SIDES
    coefficients = exact(inverse_rows[...], gathered[...])
    for side in range(SIDES):
        rows = slice(side * cap, (side + 1) * cap)
        slab = slice(side * half, (side + 1) * half)
        jump = sent[side][...] - received[side][...]
        first = 0 if stage in (2, 4) else 2
        behind = lagged(side, first, mine[slab, :], theirs[slab, :], coefficients)
        if stage == 2:
            block = 0.5 * (jump - behind)
            state = block
        elif stage == 3:
            block = (jump - behind) / theta_mid
            state = state_in[rows, :] - block
        elif stage == 4:
            block = 0.5 * (jump + behind)
            state = keep_step * state_in[rows, :] + new_step * block
        else:
            block = jump - new_step * behind
            state = state_in[rows, :] - block
        state_out[rows, :] = state
        if stage < 5:
            fill_pieces(slot_pieces, side * cap, state)
        fill_pieces(out_pieces, side * cap, block)
    copies(parts_out, components_of(own, out_pieces))
    if stage < 5:

        def write(side, block):
            outs[side][...] = block

        apply_local(matrix, codes_row, codes_lanes, slot_pieces, row_pieces, out_pieces, write)


def direct_of(modes, gathered, inverse_rows):
    coefficients = exact(inverse_rows[0:GROUP, :], gathered[...])
    return three_pass(modes[...], repeated(coefficients))


def update_kernel(stage, state, modes, gathered, inverse_rows, after, out):
    direct = direct_of(modes, gathered, inverse_rows)
    if stage == 2:
        out[...] = state[...] - direct
    elif stage == 3:
        out[...] = (state[...] - direct) / theta_mid
    else:
        out[...] = state[...] + direct


def rows_kernel(codes_lanes, residual, raw_step, start, step, modes, gathered, inverse_rows, *refs):
    targets, pieces = refs[0:3], refs[3]
    total, cols = residual.shape
    cap = total // SIDES
    direct = direct_of(modes, gathered, inverse_rows)
    multipliers = raw_step[...] - new_step * direct + start[...] + step[...]
    for n, source in enumerate((residual[...], multipliers, modes[...])):
        high, low = two_pieces(source)
        pieces[:, 2 * n * cols : (2 * n + 1) * cols] = high
        pieces[:, (2 * n + 1) * cols : (2 * n + 2) * cols] = low

    def chunk(c, carry):
        here = pl.ds(pl.multiple_of(c * cap, 16), cap)
        rows = one_pass(row_by_slot(codes_lanes[here, :], total), pieces[...])
        for n, target in enumerate(targets):
            target[here, :] = halves(rows[:, 2 * n * cols : (2 * n + 2) * cols])
        return carry

    lax.fori_loop(0, SIDES, chunk, 0)


def last_kernel(residual, modes, gathered, inverse_rows, out):
    coefficients = repeated(exact(inverse_rows[0:GROUP, :], gathered[...]))
    out[...] = residual[...] + three_pass(modes[...], coefficients)


def call(kernel, name, outs, inputs, scratch=(), smem=(), left=(), flops=None, room=58):
    spaces = [pltpu.VMEM] * len(inputs)
    for n in smem:
        spaces[n] = pltpu.SMEM
    for n in left:
        spaces[n] = pl.ANY
    shapes = []
    for shape in outs:
        shapes.append(jax.ShapeDtypeStruct(shape, jnp.float32) if isinstance(shape, tuple) else shape)
    return pl.pallas_call(
        kernel,
        name=name,
        out_shape=shapes,
        in_specs=[pl.BlockSpec(memory_space=space) for space in spaces],
        out_specs=[pl.BlockSpec(memory_space=pltpu.VMEM)] * len(outs),
        scratch_shapes=list(scratch),
        cost_estimate=None
        if flops is None
        else pl.CostEstimate(flops=flops, bytes_accessed=16 * inputs[0].size, transcendentals=0),
        compiler_params=pltpu.CompilerParams(vmem_limit_bytes=room * 1024 * 1024),
    )(*inputs)


def exchange(blocks):
    received = []
    for side, block in enumerate(blocks):
        axis = "sub" if side < 2 else "layer"
        pairs = []
        for i in range(side % 2, lax.axis_size(axis) - 1, 2):
            pairs += [(i, i + 1), (i + 1, i)]
        received.append(lax.ppermute(block, axis, pairs))
    return received


def everywhere(stacked):
    return lax.all_to_all(stacked, ("sub", "layer"), split_axis=0, concat_axis=0, tiled=True)


def per_device(
    local_gap, route_codes, flexibility, dirichlet, rigid_modes, coarse_inverse, rigid_load
):
    gap = local_gap[0, 0]
    flex = flexibility[0, 0]
    schur = dirichlet[0, 0]
    mode_count, total = rigid_modes.shape[2:]
    modes = rigid_modes.reshape(mode_count, 1, total)
    cap = total // SIDES
    cols = gap.shape[1]
    layers = lax.axis_size("layer")
    wide = lax.axis_size("sub") * layers * PAD
    pieces = pltpu.VMEM((total, 2 * cols), jnp.bfloat16)
    scratch = [pieces] * 3
    block = [(cap, cols)] * SIDES
    whole = (total, cols)
    parts = (wide, cols)
    brought = [pltpu.VMEM((total, total), jnp.float32), pltpu.SemaphoreType.DMA((SIDES,))]

    shown = call(
        functools.partial(modes_kernel, mode_count),
        "modes_to_slots",
        [(PAD, cap)] * SIDES
        + [(wide, wide + cols), jax.ShapeDtypeStruct((total, 128), jnp.int32), (2 * PAD, total)]
        + [jax.ShapeDtypeStruct((1, total), jnp.int32)],
        [route_codes[0], modes, coarse_inverse, rigid_load],
    )
    own, (inverse_load, codes_lanes, own_pieces, codes_row) = shown[:4], shown[4:]
    gathered = everywhere(inverse_load)
    partner = exchange(own)
    shown = call(
        functools.partial(operators_kernel, mode_count),
        "operators_on_modes",
        [(cap // 2, 4 * GROUP)] * SIDES + [(total, 4 * GROUP)],
        [flex, schur, codes_row, codes_lanes, *own, *partner],
        scratch + brought * 2,
        left=(0, 1),
    )
    slabs, slot_modes = shown[:4], shown[4]
    shown = call(
        functools.partial(start_kernel, mode_count, layers),
        "start",
        [(cap + cap // 2, cols)] * SIDES + [whole, (5 * GROUP, wide)],
        [flex, gap, codes_row, codes_lanes, *slabs, gathered, slot_modes],
        scratch + brought,
        left=(0,),
    )
    sent, (start, inverse_rows) = shown[:4], shown[4:]
    received = exchange(sent)
    shown = call(
        first_kernel,
        "stage_1",
        block + [whole, parts] + [(2 * cap, 4 * GROUP)] * 2,
        [schur, codes_row, codes_lanes, *received, *sent, own_pieces],
        scratch + brought,
        left=(0,),
    )
    sent, (gap_jump, components, mine, theirs) = shown[:4], shown[4:]

    def stage(number, matrix, states_in, sent, components):
        gathered = everywhere(components)
        received = exchange(sent)
        inputs = [codes_row, codes_lanes, *received, *sent, mine, theirs]
        inputs += [own_pieces, gathered, inverse_rows, *states_in]
        outs = [whole, parts]
        kernel = functools.partial(stage_kernel, number)
        name = "stage_%d" % number
        if matrix is None:
            shown = call(functools.partial(kernel, None), name, outs, inputs, scratch)
        else:
            inputs = [matrix] + inputs
            shown = call(kernel, name, block + outs, inputs, scratch + brought, left=(0,))
        return gathered, shown[:-2], *shown[-2:]

    def update(number, state, gathered, after):
        (out,) = call(
            functools.partial(update_kernel, number),
            "update_%d" % number,
            [whole],
            [state, slot_modes, gathered, inverse_rows, after],
            left=(4,),
            flops=8 * total * cols * cols,
        )
        return out

    gathered, sent, precond, components = stage(2, flex, [], sent, components)
    residual = update(2, gap_jump, gathered, components)
    gathered, sent, residual, components = stage(3, schur, [residual], sent, components)
    step = update(3, precond, gathered, components)
    gathered, sent, raw_step, components = stage(4, flex, [step], sent, components)
    residual = update(4, residual, gathered, components)
    gathered, _, residual, components = stage(5, None, [residual], sent, components)
    last_gathered = everywhere(components)
    residual, multipliers, row_modes = call(
        rows_kernel,
        "slots_to_rows",
        [whole, whole, (total, 4 * GROUP)],
        [codes_lanes, residual, raw_step, start, step, slot_modes, gathered, inverse_rows],
        [pltpu.VMEM((total, 6 * cols), jnp.bfloat16)],
    )
    gathered = last_gathered
    (residual,) = call(
        last_kernel,
        "residual",
        [whole],
        [residual, row_modes, gathered, inverse_rows],
        room=12,
    )
    return (multipliers[None, None], residual[None, None])


def solution(mesh):
    placed = (
        P("sub", "layer", None, None),
        P("sub", "layer", None),
        P("sub", "layer", None, None),
        P("sub", "layer", None, None),
        P("sub", "layer", None, None),
        P(("sub", "layer"), None),
        P(("sub", "layer"), None),
    )
    return jax.shard_map(
        per_device,
        mesh=mesh,
        in_specs=placed,
        out_specs=(P("sub", "layer", None, None), P("sub", "layer", None, None)),
        check_vma=False,
    )
```

profile of v0, /device:TPU:0, one launch (start us, length us, event | category | flops | bytes accessed | tf_op | source)
XLA Modules:
  0.0 173.1 jit_solution(799590917082309749)
XLA Ops:
  0.6 2.4 %modes_to_slots.1 = (f32[8,288]{1,0:T(8,128)}, f32[8,288]{1,0:T(8,128)}, f32[8,288]{1,0:T(8,128)}, f32[8,288]{1,0:T(8,128)}, f32[256,384]{1,0:T(8,128)}, /*index...) custom-call(s32[1,1152]{1,0:T(1,128)} %bitcast.45, f32[6,1,1152]{2,1,0:T(1,128)} %bitcast.44, ...), custom_call_target="tpu_custom_call" | custom-call | tf_op jit(solution)/shard_map/modes_to_slots/pallas_call | solution.py:400
  3.1 7.3 %all-to-all-start = ((f32[32,8,384]{2,1,0:T(8,128)}), f32[32,8,384]{2,1,0:T(8,128)S(1)}, u32[]{:S(2)}, u32[]{:S(2)}) async-start(f32[32,8,384]{2,1,0:T(8,128)} %bitcast.41), calls=%async_computation | async-start | bytes 786432 | tf_op jit(solution)/shard_map/all_to_all | solution.py:426
  10.4 1.8 %collective-permute-start = (f32[8,288]{1,0:T(8,128)}, f32[8,288]{1,0:T(8,128)S(1)}, u32[]{:S(2)}, u32[]{:S(2)}) collective-permute-start(f32[8,288]{1,0:T(8,128)} %get-tuple-element.54.refs_0_), channel_id=1, source_target_pairs={{0,4},{4,0},{8,12},{12,8},{16,20},{20,16},{24,28},{28,24},{1,5},{5... | collective-permute-start | bytes 27656 | tf_op jit(solution)/shard_map/ppermute | solution.py:421
  12.2 0.7 collective-permute-start.1
  12.9 0.7 collective-permute-start.3
  13.6 1.3 collective-permute-done.refs_4_
  15.5 10.0 %operators_on_modes.1 = (f32[144,128]{1,0:T(8,128)}, f32[144,128]{1,0:T(8,128)}, f32[144,128]{1,0:T(8,128)}, f32[144,128]{1,0:T(8,128)}, f32[1152,128]{1,0:T(8,128)}) custom-call(f32[1152,1152]{1,0:T(8,128)} %bitcast.20, f32[1152,1152]{1,0:T(8,128)} %bitcast.24, s32[1,1152]{1,0:T(1,128)} %get-tuple-element.53.codes_row, ...), custom_call_target="tpu_custom_call" | custom-call | tf_op jit(solution)/shard_map/operators_on_modes/pallas_call | solution.py:400
  25.6 0.7 copy-done.3
  26.3 7.6 %start.1 = (f32[432,128]{1,0:T(8,128)}, f32[432,128]{1,0:T(8,128)}, f32[432,128]{1,0:T(8,128)}, f32[432,128]{1,0:T(8,128)}, f32[1152,128]{1,0:T(8,128)}, /*index=5*/f32[160,256]{1,0:T(8,128)}) custom-call(f32[1152,1152]{1,0:T(8,128)} %bitcast.21, f32[1152,128]{1,0:T(8,128)} %bitcast.36, s32[1,1152]{1,0:T(1,128)} %get-tuple-element.53.codes_row, ...), custom_call_target="tpu_custom_call" | custom-call | tf_op jit(solution)/shard_map/start/pallas_call | solution.py:400
  33.9 4.5 %collective-permute-start.4 = (f32[432,128]{1,0:T(8,128)}, f32[432,128]{1,0:T(8,128)S(1)}, u32[]{:S(2)}, u32[]{:S(2)}) collective-permute-start(f32[432,128]{1,0:T(8,128)} %get-tuple-element.64.refs_4_), channel_id=1, source_target_pairs={{0,4},{4,0},{8,12},{12,8},{16,20},{20,16},{24,28},{28,24},{1,5},{5... | collective-permute-start | bytes 663560 | tf_op jit(solution)/shard_map/ppermute | solution.py:421
  38.4 0.8 collective-permute-start.5
  39.2 3.3 %collective-permute-start.6 = (f32[432,128]{1,0:T(8,128)}, f32[432,128]{1,0:T(8,128)S(1)}, u32[]{:S(2)}, u32[]{:S(2)}) collective-permute-start(f32[432,128]{1,0:T(8,128)} %get-tuple-element.66.refs_6_), channel_id=1, source_target_pairs={{0,1},{1,0},{2,3},{3,2},{4,5},{5,4},{6,7},{7,6},{8,9},{9,8},{10,11... | collective-permute-start | bytes 663560 | tf_op jit(solution)/shard_map/ppermute | solution.py:421
  42.5 0.7 collective-permute-start.7
  44.6 6.9 %stage_1.1 = (f32[288,128]{1,0:T(8,128)}, f32[288,128]{1,0:T(8,128)}, f32[288,128]{1,0:T(8,128)}, f32[288,128]{1,0:T(8,128)}, f32[1152,128]{1,0:T(8,128)}, /*ind...) custom-call(f32[1152,1152]{1,0:T(8,128)} %bitcast.25, s32[1,1152]{1,0:T(1,128)} %get-tuple-element.53.codes_row, ...), custom_call_target="tpu_custom_call" | custom-call | tf_op jit(solution)/shard_map/stage_1/pallas_call | solution.py:400
  51.5 13.2 %all-to-all-start.1 = ((f32[32,8,128]{2,1,0:T(8,128)}), f32[32,8,128]{2,1,0:T(8,128)S(1)}, u32[]{:S(2)}, u32[]{:S(2)}) async-start(f32[32,8,128]{2,1,0:T(8,128)} %bitcast.42), calls=%async_computation.1 | async-start | bytes 262144 | tf_op jit(solution)/shard_map/all_to_all | solution.py:426
  64.7 1.8 %collective-permute-start.8 = (f32[288,128]{1,0:T(8,128)}, f32[288,128]{1,0:T(8,128)S(1)}, u32[]{:S(2)}, u32[]{:S(2)}) collective-permute-start(f32[288,128]{1,0:T(8,128)} %get-tuple-element.69.refs_4_), channel_id=1, source_target_pairs={{0,4},{4,0},{8,12},{12,8},{16,20},{20,16},{24,28},{28,24},{1,5},{5... | collective-permute-start | bytes 442376 | tf_op jit(solution)/shard_map/ppermute | solution.py:421
  66.6 0.7 collective-permute-start.9
  67.3 0.7 collective-permute-start.11
  68.0 6.4 %collective-permute-done.8.refs_0_ = f32[288,128]{1,0:T(8,128)S(1)} collective-permute-done((f32[288,128]{1,0:T(8,128)}, f32[288,128]{1,0:T(8,128)S(1)}, u32[]{:S(2)}, u32[]{:S(2)}) %collective-permute-start.8) | collective-permute-done | bytes 147488 | tf_op jit(solution)/shard_map/ppermute | solution.py:421
  75.2 7.7 %stage_2.1 = (f32[288,128]{1,0:T(8,128)}, f32[288,128]{1,0:T(8,128)}, f32[288,128]{1,0:T(8,128)}, f32[288,128]{1,0:T(8,128)}, f32[1152,128]{1,0:T(8,128)}, /*index=5*/f32[256,128]{1,0:T(8,128)}) custom-call(f32[1152,1152]{1,0:T(8,128)} %bitcast.22, s32[1,1152]{1,0:T(1,128)} %get-tuple-element.53.codes_row, s32[1152,128]{1,0:T(8,128)} %get-tuple-element.52.codes_lanes, ...), custom_call_target="tpu_custom_call" | custom-call | tf_op jit(solution)/shard_map/stage_2/pallas_call | solution.py:400
  83.0 6.8 %all-to-all-start.2 = ((f32[32,8,128]{2,1,0:T(8,128)}), f32[32,8,128]{2,1,0:T(8,128)S(1)}, u32[]{:S(2)}, u32[]{:S(2)}) async-start(f32[32,8,128]{2,1,0:T(8,128)} %bitcast.39), calls=%async_computation.2 | async-start | bytes 262144 | tf_op jit(solution)/shard_map/all_to_all | solution.py:426
  89.8 1.8 %collective-permute-start.12 = (f32[288,128]{1,0:T(8,128)}, f32[288,128]{1,0:T(8,128)S(1)}, u32[]{:S(2)}, u32[]{:S(2)}) collective-permute-start(f32[288,128]{1,0:T(8,128)} %get-tuple-element.77.refs_4_), channel_id=1, source_target_pairs={{0,4},{4,0},{8,12},{12,8},{16,20},{20,16},{24,28},{28,24},{1,5},{5... | collective-permute-start | bytes 442376 | tf_op jit(solution)/shard_map/ppermute | solution.py:421
  91.6 0.7 collective-permute-start.13
  92.4 0.9 collective-permute-start.15
  93.3 2.7 %update_2.1.refs_13_ = f32[1152,128]{1,0:T(8,128)} custom-call(f32[1152,128]{1,0:T(8,128)} %get-tuple-element.82.state, f32[1152,128]{1,0:T(8,128)} %get-tuple-element.63.refs_5_.modes, f32[256,128]{1,0:T(8,128)} %bitcast.33, f32[160,256]{1,0:T(8,128)} %get-tuple-element.76.refs_12_.inverse_rows, f32[256,128]{1,0:T(8,128)} %get-tuple-element.81.after), custom_call_target="tpu_custom_call" | custom-call | flops 150994944 | bytes 2359296 | tf_op jit(solution)/shard_map/update_2/pallas_call | solution.py:400
  96.0 3.4 %collective-permute-done.12.refs_0_ = f32[288,128]{1,0:T(8,128)S(1)} collective-permute-done((f32[288,128]{1,0:T(8,128)}, f32[288,128]{1,0:T(8,128)S(1)}, u32[]{:S(2)}, u32[]{:S(2)}) %collective-permute-start.12) | collective-permute-done | bytes 147488 | tf_op jit(solution)/shard_map/ppermute | solution.py:421
  99.5 0.6 copy-done.16
  100.3 7.9 %stage_3.1 = (f32[288,128]{1,0:T(8,128)}, f32[288,128]{1,0:T(8,128)}, f32[288,128]{1,0:T(8,128)}, f32[288,128]{1,0:T(8,128)}, f32[1152,128]{1,0:T(8,128)}, /*index=5*/f32[256,128]{1,0:T(8,128)}) custom-call(f32[1152,1152]{1,0:T(8,128)} %bitcast.26, s32[1,1152]{1,0:T(1,128)} %get-tuple-element.53.codes_row, s32[1152,128]{1,0:T(8,128)} %get-tuple-element.52.codes_lanes, ...), custom_call_target="tpu_custom_call" | custom-call | tf_op jit(solution)/shard_map/stage_3/pallas_call | solution.py:400
  108.1 6.8 %all-to-all-start.3 = ((f32[32,8,128]{2,1,0:T(8,128)}), f32[32,8,128]{2,1,0:T(8,128)S(1)}, u32[]{:S(2)}, u32[]{:S(2)}) async-start(f32[32,8,128]{2,1,0:T(8,128)} %bitcast.38), calls=%async_computation.3 | async-start | bytes 262144 | tf_op jit(solution)/shard_map/all_to_all | solution.py:426
  115.0 1.8 %collective-permute-start.16 = (f32[288,128]{1,0:T(8,128)}, f32[288,128]{1,0:T(8,128)S(1)}, u32[]{:S(2)}, u32[]{:S(2)}) collective-permute-start(f32[288,128]{1,0:T(8,128)} %get-tuple-element.83.refs_4_), channel_id=1, source_target_pairs={{0,4},{4,0},{8,12},{12,8},{16,20},{20,16},{24,28},{28,24},{1,5},{5... | collective-permute-start | bytes 442376 | tf_op jit(solution)/shard_map/ppermute | solution.py:421
  116.8 0.7 collective-permute-start.17
  117.6 0.7 collective-permute-start.19
  118.2 2.7 %update_3.1.refs_13_.step = f32[1152,128]{1,0:T(8,128)} custom-call(f32[1152,128]{1,0:T(8,128)} %get-tuple-element.88.state, f32[1152,128]{1,0:T(8,128)} %get-tuple-element.63.refs_5_.modes, f32[256,128]{1,0:T(8,128)} %bitcast.29, f32[160,256]{1,0:T(8,128)} %get-tuple-element.76.refs_12_.inverse_rows, f32[256,128]{1,0:T(8,128)} %get-tuple-element.87.after), custom_call_target="tpu_custom_call" | custom-call | flops 150994944 | bytes 2359296 | tf_op jit(solution)/shard_map/update_3/pallas_call | solution.py:400
  120.9 3.6 %collective-permute-done.16.refs_0_ = f32[288,128]{1,0:T(8,128)S(1)} collective-permute-done((f32[288,128]{1,0:T(8,128)}, f32[288,128]{1,0:T(8,128)S(1)}, u32[]{:S(2)}, u32[]{:S(2)}) %collective-permute-start.16) | collective-permute-done | bytes 147488 | tf_op jit(solution)/shard_map/ppermute | solution.py:421
  125.5 7.9 %stage_4.1 = (f32[288,128]{1,0:T(8,128)}, f32[288,128]{1,0:T(8,128)}, f32[288,128]{1,0:T(8,128)}, f32[288,128]{1,0:T(8,128)}, f32[1152,128]{1,0:T(8,128)}, /*index=5*/f32[256,128]{1,0:T(8,128)}) custom-call(f32[1152,1152]{1,0:T(8,128)} %bitcast.23, s32[1,1152]{1,0:T(1,128)} %get-tuple-element.53.codes_row, s32[1152,128]{1,0:T(8,128)} %get-tuple-element.52.codes_lanes, ...), custom_call_target="tpu_custom_call" | custom-call | tf_op jit(solution)/shard_map/stage_4/pallas_call | solution.py:400
  133.4 6.8 %all-to-all-start.4 = ((f32[32,8,128]{2,1,0:T(8,128)}), f32[32,8,128]{2,1,0:T(8,128)S(1)}, u32[]{:S(2)}, u32[]{:S(2)}) async-start(f32[32,8,128]{2,1,0:T(8,128)} %bitcast.40), calls=%async_computation.4 | async-start | bytes 262144 | tf_op jit(solution)/shard_map/all_to_all | solution.py:426
  140.2 1.8 %collective-permute-start.20 = (f32[288,128]{1,0:T(8,128)}, f32[288,128]{1,0:T(8,128)S(1)}, u32[]{:S(2)}, u32[]{:S(2)}) collective-permute-start(f32[288,128]{1,0:T(8,128)} %get-tuple-element.89.refs_4_), channel_id=1, source_target_pairs={{0,4},{4,0},{8,12},{12,8},{16,20},{20,16},{24,28},{28,24},{1,5},{5... | collective-permute-start | bytes 442376 | tf_op jit(solution)/shard_map/ppermute | solution.py:421
  142.0 0.7 collective-permute-start.21
  142.8 0.7 collective-permute-start.23
  143.4 2.7 %update_4.1.refs_13_ = f32[1152,128]{1,0:T(8,128)} custom-call(f32[1152,128]{1,0:T(8,128)} %get-tuple-element.94.state, f32[1152,128]{1,0:T(8,128)} %get-tuple-element.63.refs_5_.modes, f32[256,128]{1,0:T(8,128)} %bitcast.31, f32[160,256]{1,0:T(8,128)} %get-tuple-element.76.refs_12_.inverse_rows, f32[256,128]{1,0:T(8,128)} %get-tuple-element.93.after), custom_call_target="tpu_custom_call" | custom-call | flops 150994944 | bytes 2359296 | tf_op jit(solution)/shard_map/update_4/pallas_call | solution.py:400
  146.2 3.6 %collective-permute-done.20.refs_0_ = f32[288,128]{1,0:T(8,128)S(1)} collective-permute-done((f32[288,128]{1,0:T(8,128)}, f32[288,128]{1,0:T(8,128)S(1)}, u32[]{:S(2)}, u32[]{:S(2)}) %collective-permute-start.20) | collective-permute-done | bytes 147488 | tf_op jit(solution)/shard_map/ppermute | solution.py:421
  150.6 3.9 %stage_5.1 = (f32[1152,128]{1,0:T(8,128)}, f32[256,128]{1,0:T(8,128)}) custom-call(s32[1,1152]{1,0:T(1,128)} %get-tuple-element.53.codes_row, s32[1152,128]{1,0:T(8,128)} %get-tuple-element.52.codes_lanes, f32[288,128]{1,0:T(8,128)} %copy-done.12, f32[288,128]{1,0:T(8,128)} %copy-done.13, f32[288,128]{1,0:T(8,128)} %copy-done.14, f32[288,128]{1,0:T(8,128)} %copy-done.15, ...), custom_call_target="tpu_custom_call" | custom-call | tf_op jit(solution)/shard_map/stage_5/pallas_call | solution.py:400
  154.5 6.8 %all-to-all-start.5 = ((f32[32,8,128]{2,1,0:T(8,128)}), f32[32,8,128]{2,1,0:T(8,128)S(1)}, u32[]{:S(2)}, u32[]{:S(2)}) async-start(f32[32,8,128]{2,1,0:T(8,128)} %bitcast.43), calls=%async_computation.5 | async-start | bytes 262144 | tf_op jit(solution)/shard_map/all_to_all | solution.py:426
  161.4 6.8 %slots_to_rows.1 = (f32[1152,128]{1,0:T(8,128)}, f32[1152,128]{1,0:T(8,128)}, f32[1152,128]{1,0:T(8,128)}) custom-call(s32[1152,128]{1,0:T(8,128)} %get-tuple-element.52.codes_lanes, f32[1152,128]{1,0:T(8,128)} %get-tuple-element.95.residual, f32[1152,128]{1,0:T(8,128)} %get-tuple-element.96.raw_step, f32[1152,128]{1,0:T(8,128)} %get-tuple-element.97.start, ...), custom_call_target="tpu_custom_call" | custom-call | tf_op jit(solution)/shard_map/slots_to_rows/pallas_call | solution.py:400
  168.2 1.4 all-to-all-done.5
  169.6 1.1 copy-done.1
  170.7 1.1 copy-done.2
  171.7 1.4 residual.1
  (89 shorter events, 5.0 us)
Async XLA Ops:
  3.1 22.5 %all-to-all-start = ((f32[32,8,384]{2,1,0:T(8,128)}), f32[32,8,384]{2,1,0:T(8,128)S(1)}, u32[]{:S(2)}, u32[]{:S(2)}) async-start(f32[32,8,384]{2,1,0:T(8,128)} %bitcast.41), calls=%async_computation | async-start | bytes 786432 | tf_op jit(solution)/shard_map/all_to_all | solution.py:426
  10.4 4.5 %collective-permute-start = (f32[8,288]{1,0:T(8,128)}, f32[8,288]{1,0:T(8,128)S(1)}, u32[]{:S(2)}, u32[]{:S(2)}) collective-permute-start(f32[8,288]{1,0:T(8,128)} %get-tuple-element.54.refs_0_), channel_id=1, source_target_pairs={{0,4},{4,0},{8,12},{12,8},{16,20},{20,16},{24,28},{28,24},{1,5},{5... | collective-permute-start | bytes 27656 | tf_op jit(solution)/shard_map/ppermute | solution.py:421
  12.2 2.7 %collective-permute-start.1 = (f32[8,288]{1,0:T(8,128)}, f32[8,288]{1,0:T(8,128)S(1)}, u32[]{:S(2)}, u32[]{:S(2)}) collective-permute-start(f32[8,288]{1,0:T(8,128)} %get-tuple-element.55.refs_1_), channel_id=1, source_target_pairs={{4,8},{8,4},{12,16},{16,12},{20,24},{24,20},{5,9},{9,5},{13,17},{1... | collective-permute-start | bytes 27656 | tf_op jit(solution)/shard_map/ppermute | solution.py:421
  12.8 2.1 %collective-permute-start.2 = (f32[8,288]{1,0:T(8,128)}, f32[8,288]{1,0:T(8,128)S(1)}, u32[]{:S(2)}, u32[]{:S(2)}) collective-permute-start(f32[8,288]{1,0:T(8,128)} %get-tuple-element.56.refs_2_), channel_id=1, source_target_pairs={{0,1},{1,0},{2,3},{3,2},{4,5},{5,4},{6,7},{7,6},{8,9},{9,8},{10,11... | collective-permute-start | bytes 27656 | tf_op jit(solution)/shard_map/ppermute | solution.py:421
  12.9 2.0 %collective-permute-start.3 = (f32[8,288]{1,0:T(8,128)}, f32[8,288]{1,0:T(8,128)S(1)}, u32[]{:S(2)}, u32[]{:S(2)}) collective-permute-start(f32[8,288]{1,0:T(8,128)} %get-tuple-element.57.refs_3_), channel_id=1, source_target_pairs={{1,2},{2,1},{5,6},{6,5},{9,10},{10,9},{13,14},{14,13},{17,18},{18,... | collective-permute-start | bytes 27656 | tf_op jit(solution)/shard_map/ppermute | solution.py:421
  25.6 0.7 copy-start.3
  33.9 9.3 %collective-permute-start.4 = (f32[432,128]{1,0:T(8,128)}, f32[432,128]{1,0:T(8,128)S(1)}, u32[]{:S(2)}, u32[]{:S(2)}) collective-permute-start(f32[432,128]{1,0:T(8,128)} %get-tuple-element.64.refs_4_), channel_id=1, source_target_pairs={{0,4},{4,0},{8,12},{12,8},{16,20},{20,16},{24,28},{28,24},{1,5},{5... | collective-permute-start | bytes 663560 | tf_op jit(solution)/shard_map/ppermute | solution.py:421
  38.4 4.8 %collective-permute-start.5 = (f32[432,128]{1,0:T(8,128)}, f32[432,128]{1,0:T(8,128)S(1)}, u32[]{:S(2)}, u32[]{:S(2)}) collective-permute-start(f32[432,128]{1,0:T(8,128)} %get-tuple-element.65.refs_5_), channel_id=1, source_target_pairs={{4,8},{8,4},{12,16},{16,12},{20,24},{24,20},{5,9},{9,5},{13,17},{1... | collective-permute-start | bytes 663560 | tf_op jit(solution)/shard_map/ppermute | solution.py:421
  39.2 4.6 %collective-permute-start.6 = (f32[432,128]{1,0:T(8,128)}, f32[432,128]{1,0:T(8,128)S(1)}, u32[]{:S(2)}, u32[]{:S(2)}) collective-permute-start(f32[432,128]{1,0:T(8,128)} %get-tuple-element.66.refs_6_), channel_id=1, source_target_pairs={{0,1},{1,0},{2,3},{3,2},{4,5},{5,4},{6,7},{7,6},{8,9},{9,8},{10,11... | collective-permute-start | bytes 663560 | tf_op jit(solution)/shard_map/ppermute | solution.py:421
  42.5 1.3 collective-permute-start.7
  43.2 0.7 copy-start.9
  43.8 0.8 copy-start.11
  51.5 22.9 %all-to-all-start.1 = ((f32[32,8,128]{2,1,0:T(8,128)}), f32[32,8,128]{2,1,0:T(8,128)S(1)}, u32[]{:S(2)}, u32[]{:S(2)}) async-start(f32[32,8,128]{2,1,0:T(8,128)} %bitcast.42), calls=%async_computation.1 | async-start | bytes 262144 | tf_op jit(solution)/shard_map/all_to_all | solution.py:426
  64.7 9.6 %collective-permute-start.8 = (f32[288,128]{1,0:T(8,128)}, f32[288,128]{1,0:T(8,128)S(1)}, u32[]{:S(2)}, u32[]{:S(2)}) collective-permute-start(f32[288,128]{1,0:T(8,128)} %get-tuple-element.69.refs_4_), channel_id=1, source_target_pairs={{0,4},{4,0},{8,12},{12,8},{16,20},{20,16},{24,28},{28,24},{1,5},{5... | collective-permute-start | bytes 442376 | tf_op jit(solution)/shard_map/ppermute | solution.py:421
  66.6 7.8 %collective-permute-start.9 = (f32[288,128]{1,0:T(8,128)}, f32[288,128]{1,0:T(8,128)S(1)}, u32[]{:S(2)}, u32[]{:S(2)}) collective-permute-start(f32[288,128]{1,0:T(8,128)} %get-tuple-element.70.refs_5_), channel_id=1, source_target_pairs={{4,8},{8,4},{12,16},{16,12},{20,24},{24,20},{5,9},{9,5},{13,17},{1... | collective-permute-start | bytes 442376 | tf_op jit(solution)/shard_map/ppermute | solution.py:421
  67.2 7.1 %collective-permute-start.10 = (f32[288,128]{1,0:T(8,128)}, f32[288,128]{1,0:T(8,128)S(1)}, u32[]{:S(2)}, u32[]{:S(2)}) collective-permute-start(f32[288,128]{1,0:T(8,128)} %get-tuple-element.71.refs_6_), channel_id=1, source_target_pairs={{0,1},{1,0},{2,3},{3,2},{4,5},{5,4},{6,7},{7,6},{8,9},{9,8},{10,11... | collective-permute-start | bytes 442376 | tf_op jit(solution)/shard_map/ppermute | solution.py:421
  67.3 7.1 %collective-permute-start.11 = (f32[288,128]{1,0:T(8,128)}, f32[288,128]{1,0:T(8,128)S(1)}, u32[]{:S(2)}, u32[]{:S(2)}) collective-permute-start(f32[288,128]{1,0:T(8,128)} %get-tuple-element.72.refs_7_), channel_id=1, source_target_pairs={{1,2},{2,1},{5,6},{6,5},{9,10},{10,9},{13,14},{14,13},{17,18},{18,... | collective-permute-start | bytes 442376 | tf_op jit(solution)/shard_map/ppermute | solution.py:421
  74.4 0.8 copy-start.26
  74.4 0.8 copy-start.27
  74.4 0.8 copy-start.6
  83.0 16.5 %all-to-all-start.2 = ((f32[32,8,128]{2,1,0:T(8,128)}), f32[32,8,128]{2,1,0:T(8,128)S(1)}, u32[]{:S(2)}, u32[]{:S(2)}) async-start(f32[32,8,128]{2,1,0:T(8,128)} %bitcast.39), calls=%async_computation.2 | async-start | bytes 262144 | tf_op jit(solution)/shard_map/all_to_all | solution.py:426
  89.8 9.6 %collective-permute-start.12 = (f32[288,128]{1,0:T(8,128)}, f32[288,128]{1,0:T(8,128)S(1)}, u32[]{:S(2)}, u32[]{:S(2)}) collective-permute-start(f32[288,128]{1,0:T(8,128)} %get-tuple-element.77.refs_4_), channel_id=1, source_target_pairs={{0,4},{4,0},{8,12},{12,8},{16,20},{20,16},{24,28},{28,24},{1,5},{5... | collective-permute-start | bytes 442376 | tf_op jit(solution)/shard_map/ppermute | solution.py:421
  91.6 7.8 %collective-permute-start.13 = (f32[288,128]{1,0:T(8,128)}, f32[288,128]{1,0:T(8,128)S(1)}, u32[]{:S(2)}, u32[]{:S(2)}) collective-permute-start(f32[288,128]{1,0:T(8,128)} %get-tuple-element.78.refs_5_), channel_id=1, source_target_pairs={{4,8},{8,4},{12,16},{16,12},{20,24},{24,20},{5,9},{9,5},{13,17},{1... | collective-permute-start | bytes 442376 | tf_op jit(solution)/shard_map/ppermute | solution.py:421
  92.3 7.1 %collective-permute-start.14 = (f32[288,128]{1,0:T(8,128)}, f32[288,128]{1,0:T(8,128)S(1)}, u32[]{:S(2)}, u32[]{:S(2)}) collective-permute-start(f32[288,128]{1,0:T(8,128)} %get-tuple-element.79.refs_6_), channel_id=1, source_target_pairs={{0,1},{1,0},{2,3},{3,2},{4,5},{5,4},{6,7},{7,6},{8,9},{9,8},{10,11... | collective-permute-start | bytes 442376 | tf_op jit(solution)/shard_map/ppermute | solution.py:421
  92.4 7.1 %collective-permute-start.15 = (f32[288,128]{1,0:T(8,128)}, f32[288,128]{1,0:T(8,128)S(1)}, u32[]{:S(2)}, u32[]{:S(2)}) collective-permute-start(f32[288,128]{1,0:T(8,128)} %get-tuple-element.80.refs_7_), channel_id=1, source_target_pairs={{1,2},{2,1},{5,6},{6,5},{9,10},{10,9},{13,14},{14,13},{17,18},{18,... | collective-permute-start | bytes 442376 | tf_op jit(solution)/shard_map/ppermute | solution.py:421
  99.4 0.8 copy-start.21
  99.4 0.8 copy-start.24
  99.5 0.8 copy-start.4
  108.1 16.5 %all-to-all-start.3 = ((f32[32,8,128]{2,1,0:T(8,128)}), f32[32,8,128]{2,1,0:T(8,128)S(1)}, u32[]{:S(2)}, u32[]{:S(2)}) async-start(f32[32,8,128]{2,1,0:T(8,128)} %bitcast.38), calls=%async_computation.3 | async-start | bytes 262144 | tf_op jit(solution)/shard_map/all_to_all | solution.py:426
  115.0 9.6 %collective-permute-start.16 = (f32[288,128]{1,0:T(8,128)}, f32[288,128]{1,0:T(8,128)S(1)}, u32[]{:S(2)}, u32[]{:S(2)}) collective-permute-start(f32[288,128]{1,0:T(8,128)} %get-tuple-element.83.refs_4_), channel_id=1, source_target_pairs={{0,4},{4,0},{8,12},{12,8},{16,20},{20,16},{24,28},{28,24},{1,5},{5... | collective-permute-start | bytes 442376 | tf_op jit(solution)/shard_map/ppermute | solution.py:421
  116.8 7.8 %collective-permute-start.17 = (f32[288,128]{1,0:T(8,128)}, f32[288,128]{1,0:T(8,128)S(1)}, u32[]{:S(2)}, u32[]{:S(2)}) collective-permute-start(f32[288,128]{1,0:T(8,128)} %get-tuple-element.84.refs_5_), channel_id=1, source_target_pairs={{4,8},{8,4},{12,16},{16,12},{20,24},{24,20},{5,9},{9,5},{13,17},{1... | collective-permute-start | bytes 442376 | tf_op jit(solution)/shard_map/ppermute | solution.py:421
  117.5 7.1 %collective-permute-start.18 = (f32[288,128]{1,0:T(8,128)}, f32[288,128]{1,0:T(8,128)S(1)}, u32[]{:S(2)}, u32[]{:S(2)}) collective-permute-start(f32[288,128]{1,0:T(8,128)} %get-tuple-element.85.refs_6_), channel_id=1, source_target_pairs={{0,1},{1,0},{2,3},{3,2},{4,5},{5,4},{6,7},{7,6},{8,9},{9,8},{10,11... | collective-permute-start | bytes 442376 | tf_op jit(solution)/shard_map/ppermute | solution.py:421
  117.6 7.1 %collective-permute-start.19 = (f32[288,128]{1,0:T(8,128)}, f32[288,128]{1,0:T(8,128)S(1)}, u32[]{:S(2)}, u32[]{:S(2)}) collective-permute-start(f32[288,128]{1,0:T(8,128)} %get-tuple-element.86.refs_7_), channel_id=1, source_target_pairs={{1,2},{2,1},{5,6},{6,5},{9,10},{10,9},{13,14},{14,13},{17,18},{18,... | collective-permute-start | bytes 442376 | tf_op jit(solution)/shard_map/ppermute | solution.py:421
  124.6 0.8 copy-start.22
  124.6 0.8 copy-start.25
  124.6 0.8 copy-start.5
  133.3 36.3 %copy-start = (f32[160,256]{1,0:T(8,128)S(1)}, f32[160,256]{1,0:T(8,128)}, u32[]{:S(2)}) copy-start(f32[160,256]{1,0:T(8,128)} %get-tuple-element.76.refs_12_.inverse_rows) | copy-start | bytes 491524
  133.4 16.5 %all-to-all-start.4 = ((f32[32,8,128]{2,1,0:T(8,128)}), f32[32,8,128]{2,1,0:T(8,128)S(1)}, u32[]{:S(2)}, u32[]{:S(2)}) async-start(f32[32,8,128]{2,1,0:T(8,128)} %bitcast.40), calls=%async_computation.4 | async-start | bytes 262144 | tf_op jit(solution)/shard_map/all_to_all | solution.py:426
  140.2 9.6 %collective-permute-start.20 = (f32[288,128]{1,0:T(8,128)}, f32[288,128]{1,0:T(8,128)S(1)}, u32[]{:S(2)}, u32[]{:S(2)}) collective-permute-start(f32[288,128]{1,0:T(8,128)} %get-tuple-element.89.refs_4_), channel_id=1, source_target_pairs={{0,4},{4,0},{8,12},{12,8},{16,20},{20,16},{24,28},{28,24},{1,5},{5... | collective-permute-start | bytes 442376 | tf_op jit(solution)/shard_map/ppermute | solution.py:421
  142.0 7.8 %collective-permute-start.21 = (f32[288,128]{1,0:T(8,128)}, f32[288,128]{1,0:T(8,128)S(1)}, u32[]{:S(2)}, u32[]{:S(2)}) collective-permute-start(f32[288,128]{1,0:T(8,128)} %get-tuple-element.90.refs_5_), channel_id=1, source_target_pairs={{4,8},{8,4},{12,16},{16,12},{20,24},{24,20},{5,9},{9,5},{13,17},{1... | collective-permute-start | bytes 442376 | tf_op jit(solution)/shard_map/ppermute | solution.py:421
  142.7 7.1 %collective-permute-start.22 = (f32[288,128]{1,0:T(8,128)}, f32[288,128]{1,0:T(8,128)S(1)}, u32[]{:S(2)}, u32[]{:S(2)}) collective-permute-start(f32[288,128]{1,0:T(8,128)} %get-tuple-element.91.refs_6_), channel_id=1, source_target_pairs={{0,1},{1,0},{2,3},{3,2},{4,5},{5,4},{6,7},{7,6},{8,9},{9,8},{10,11... | collective-permute-start | bytes 442376 | tf_op jit(solution)/shard_map/ppermute | solution.py:421
  142.8 7.1 %collective-permute-start.23 = (f32[288,128]{1,0:T(8,128)}, f32[288,128]{1,0:T(8,128)S(1)}, u32[]{:S(2)}, u32[]{:S(2)}) collective-permute-start(f32[288,128]{1,0:T(8,128)} %get-tuple-element.92.refs_7_), channel_id=1, source_target_pairs={{1,2},{2,1},{5,6},{6,5},{9,10},{10,9},{13,14},{14,13},{17,18},{18,... | collective-permute-start | bytes 442376 | tf_op jit(solution)/shard_map/ppermute | solution.py:421
  149.8 0.7 copy-start.14
  149.8 0.8 copy-start.15
  149.8 0.8 copy-start.7
  154.5 15.1 %all-to-all-start.5 = ((f32[32,8,128]{2,1,0:T(8,128)}), f32[32,8,128]{2,1,0:T(8,128)S(1)}, u32[]{:S(2)}, u32[]{:S(2)}) async-start(f32[32,8,128]{2,1,0:T(8,128)} %bitcast.43), calls=%async_computation.5 | async-start | bytes 262144 | tf_op jit(solution)/shard_map/all_to_all | solution.py:426
  169.6 1.1 copy-start.1
  170.7 1.1 copy-start.2
  (14 other events, 9.3 us)
where the time goes:
time: 174 us; the launch traced here: 173 us
  starting transfers between devices  73.5 us (42%)
  Pallas kernels  70.7 us (41%)
  waiting for transfers between devices  20.4 us (12%)
  local copies, waits for them, and re-layouts  7.43 us (4%)
    pallas_call x13, Pallas kernels, call(): pl.pallas_call(kernel, name=name, out_shape=shapes, in_specs=[pl.BlockSpe...  70.7 us
    all_to_all x6, starting transfers between devices, everywhere(): lax.all_to_all(stacked, ('sub', 'layer'), split_axis=0, concat_axis=0, ti...  47.9 us
    ppermute x24, starting transfers between devices, exchange(): received.append(lax.ppermute(block, axis, pairs))  25.6 us
    ppermute x24, waiting for transfers between devices, exchange(): received.append(lax.ppermute(block, axis, pairs))  19 us
    unnamed x64, local copies, waits for them, and re-layouts  7.43 us
  transfers between devices with their start and end apart: 30, of which 7 were waited for; matrix products, arithmetic and copies ran while one was open for 0% of the time, Pallas kernels for 14%

commit v1 on v0

--- a/solution.py
+++ b/solution.py
@@ -315,7 +315,7 @@
     total = codes_lanes.shape[0]
     cap = total // SIDES
     half = mine.shape[0] // SIDES
-    coefficients = exact(inverse_rows[...], gathered[...])
+    coefficients = three_pass(inverse_rows[...], gathered[...])
     for side in range(SIDES):
         rows = slice(side * cap, (side + 1) * cap)
         slab = slice(side * half, (side + 1) * half)
@@ -348,7 +348,7 @@
 
 
 def direct_of(modes, gathered, inverse_rows):
-    coefficients = exact(inverse_rows[0:GROUP, :], gathered[...])
+    coefficients = three_pass(inverse_rows[0:GROUP, :], gathered[...])
     return three_pass(modes[...], repeated(coefficients))
 
 
@@ -384,7 +384,7 @@
 
 
 def last_kernel(residual, modes, gathered, inverse_rows, out):
-    coefficients = repeated(exact(inverse_rows[0:GROUP, :], gathered[...]))
+    coefficients = repeated(three_pass(inverse_rows[0:GROUP, :], gathered[...]))
     out[...] = residual[...] + three_pass(modes[...], coefficients)
 
 
@@ -532,7 +532,6 @@
         "residual",
         [whole],
         [residual, row_modes, gathered, inverse_rows],
-        room=12,
     )
     return (multipliers[None, None], residual[None, None])
 

time: 174 us -> 173 us (level)
    unnamed x64 -> x60, local copies, waits for them, and re-layouts: 7.43 us -> 5.97 us
where the time goes in v1:
time: 173 us; the launch traced here: 172 us
  starting transfers between devices  73.5 us (42%)
  Pallas kernels  70.4 us (41%)
  waiting for transfers between devices  20.6 us (12%)
  local copies, waits for them, and re-layouts  5.97 us (3%)
    pallas_call x13, Pallas kernels, call(): pl.pallas_call(kernel, name=name, out_shape=shapes, in_specs=[pl.BlockSpe...  70.4 us
    all_to_all x6, starting transfers between devices, everywhere(): lax.all_to_all(stacked, ('sub', 'layer'), split_axis=0, concat_axis=0, ti...  47.9 us
    ppermute x24, starting transfers between devices, exchange(): received.append(lax.ppermute(block, axis, pairs))  25.6 us
    ppermute x24, waiting for transfers between devices, exchange(): received.append(lax.ppermute(block, axis, pairs))  19.1 us
    unnamed x60, local copies, waits for them, and re-layouts  5.97 us
  transfers between devices with their start and end apart: 30, of which 7 were waited for; matrix products, arithmetic and copies ran while one was open for 0% of the time, Pallas kernels for 14%

profile of v1, /device:TPU:0, one launch (start us, length us, event | category | flops | bytes accessed | tf_op | source)
XLA Modules:
  0.0 171.5 jit_solution(13609476236659296727)
XLA Ops:
  0.6 2.4 %modes_to_slots.1 = (f32[8,288]{1,0:T(8,128)}, f32[8,288]{1,0:T(8,128)}, f32[8,288]{1,0:T(8,128)}, f32[8,288]{1,0:T(8,128)}, f32[256,384]{1,0:T(8,128)}, /*index...) custom-call(s32[1,1152]{1,0:T(1,128)} %bitcast.45, f32[6,1,1152]{2,1,0:T(1,128)} %bitcast.44, ...), custom_call_target="tpu_custom_call" | custom-call | tf_op jit(solution)/shard_map/modes_to_slots/pallas_call | solution.py:400
  3.1 7.3 %all-to-all-start = ((f32[32,8,384]{2,1,0:T(8,128)}), f32[32,8,384]{2,1,0:T(8,128)S(1)}, u32[]{:S(2)}, u32[]{:S(2)}) async-start(f32[32,8,384]{2,1,0:T(8,128)} %bitcast.41), calls=%async_computation | async-start | bytes 786432 | tf_op jit(solution)/shard_map/all_to_all | solution.py:426
  10.4 1.8 %collective-permute-start = (f32[8,288]{1,0:T(8,128)}, f32[8,288]{1,0:T(8,128)S(1)}, u32[]{:S(2)}, u32[]{:S(2)}) collective-permute-start(f32[8,288]{1,0:T(8,128)} %get-tuple-element.54.refs_0_), channel_id=1, source_target_pairs={{0,4},{4,0},{8,12},{12,8},{16,20},{20,16},{24,28},{28,24},{1,5},{5... | collective-permute-start | bytes 27656 | tf_op jit(solution)/shard_map/ppermute | solution.py:421
  12.2 0.7 collective-permute-start.1
  12.9 0.7 collective-permute-start.3
  13.6 1.3 collective-permute-done.refs_4_
  15.5 10.0 %operators_on_modes.1 = (f32[144,128]{1,0:T(8,128)}, f32[144,128]{1,0:T(8,128)}, f32[144,128]{1,0:T(8,128)}, f32[144,128]{1,0:T(8,128)}, f32[1152,128]{1,0:T(8,128)}) custom-call(f32[1152,1152]{1,0:T(8,128)} %bitcast.19, f32[1152,1152]{1,0:T(8,128)} %bitcast.23, s32[1,1152]{1,0:T(1,128)} %get-tuple-element.53.codes_row, ...), custom_call_target="tpu_custom_call" | custom-call | tf_op jit(solution)/shard_map/operators_on_modes/pallas_call | solution.py:400
  25.6 0.7 copy-done
  26.3 7.6 %start.1 = (f32[432,128]{1,0:T(8,128)}, f32[432,128]{1,0:T(8,128)}, f32[432,128]{1,0:T(8,128)}, f32[432,128]{1,0:T(8,128)}, f32[1152,128]{1,0:T(8,128)}, /*index=5*/f32[160,256]{1,0:T(8,128)}) custom-call(f32[1152,1152]{1,0:T(8,128)} %bitcast.20, f32[1152,128]{1,0:T(8,128)} %bitcast.35, s32[1,1152]{1,0:T(1,128)} %get-tuple-element.53.codes_row, ...), custom_call_target="tpu_custom_call" | custom-call | tf_op jit(solution)/shard_map/start/pallas_call | solution.py:400
  33.9 4.5 %collective-permute-start.4 = (f32[432,128]{1,0:T(8,128)}, f32[432,128]{1,0:T(8,128)S(1)}, u32[]{:S(2)}, u32[]{:S(2)}) collective-permute-start(f32[432,128]{1,0:T(8,128)} %get-tuple-element.64.refs_4_), channel_id=1, source_target_pairs={{0,4},{4,0},{8,12},{12,8},{16,20},{20,16},{24,28},{28,24},{1,5},{5... | collective-permute-start | bytes 663560 | tf_op jit(solution)/shard_map/ppermute | solution.py:421
  38.4 0.8 collective-permute-start.5
  39.3 3.3 %collective-permute-start.6 = (f32[432,128]{1,0:T(8,128)}, f32[432,128]{1,0:T(8,128)S(1)}, u32[]{:S(2)}, u32[]{:S(2)}) collective-permute-start(f32[432,128]{1,0:T(8,128)} %get-tuple-element.66.refs_6_), channel_id=1, source_target_pairs={{0,1},{1,0},{2,3},{3,2},{4,5},{5,4},{6,7},{7,6},{8,9},{9,8},{10,11... | collective-permute-start | bytes 663560 | tf_op jit(solution)/shard_map/ppermute | solution.py:421
  42.5 0.7 collective-permute-start.7
  43.2 0.6 collective-permute-done.6.refs_2_
  44.6 6.9 %stage_1.1 = (f32[288,128]{1,0:T(8,128)}, f32[288,128]{1,0:T(8,128)}, f32[288,128]{1,0:T(8,128)}, f32[288,128]{1,0:T(8,128)}, f32[1152,128]{1,0:T(8,128)}, /*ind...) custom-call(f32[1152,1152]{1,0:T(8,128)} %bitcast.24, s32[1,1152]{1,0:T(1,128)} %get-tuple-element.53.codes_row, ...), custom_call_target="tpu_custom_call" | custom-call | tf_op jit(solution)/shard_map/stage_1/pallas_call | solution.py:400
  51.5 13.2 %all-to-all-start.1 = ((f32[32,8,128]{2,1,0:T(8,128)}), f32[32,8,128]{2,1,0:T(8,128)S(1)}, u32[]{:S(2)}, u32[]{:S(2)}) async-start(f32[32,8,128]{2,1,0:T(8,128)} %bitcast.42), calls=%async_computation.1 | async-start | bytes 262144 | tf_op jit(solution)/shard_map/all_to_all | solution.py:426
  64.8 1.8 %collective-permute-start.8 = (f32[288,128]{1,0:T(8,128)}, f32[288,128]{1,0:T(8,128)S(1)}, u32[]{:S(2)}, u32[]{:S(2)}) collective-permute-start(f32[288,128]{1,0:T(8,128)} %get-tuple-element.69.refs_4_), channel_id=1, source_target_pairs={{0,4},{4,0},{8,12},{12,8},{16,20},{20,16},{24,28},{28,24},{1,5},{5... | collective-permute-start | bytes 442376 | tf_op jit(solution)/shard_map/ppermute | solution.py:421
  66.6 0.7 collective-permute-start.9
  67.4 0.7 collective-permute-start.11
  68.0 6.4 %collective-permute-done.8.refs_0_ = f32[288,128]{1,0:T(8,128)S(1)} collective-permute-done((f32[288,128]{1,0:T(8,128)}, f32[288,128]{1,0:T(8,128)S(1)}, u32[]{:S(2)}, u32[]{:S(2)}) %collective-permute-start.8) | collective-permute-done | bytes 147488 | tf_op jit(solution)/shard_map/ppermute | solution.py:421
  75.2 7.3 %stage_2.1 = (f32[288,128]{1,0:T(8,128)}, f32[288,128]{1,0:T(8,128)}, f32[288,128]{1,0:T(8,128)}, f32[288,128]{1,0:T(8,128)}, f32[1152,128]{1,0:T(8,128)}, /*index=5*/f32[256,128]{1,0:T(8,128)}) custom-call(f32[1152,1152]{1,0:T(8,128)} %bitcast.21, s32[1,1152]{1,0:T(1,128)} %get-tuple-element.53.codes_row, s32[1152,128]{1,0:T(8,128)} %get-tuple-element.52.codes_lanes, ...), custom_call_target="tpu_custom_call" | custom-call | tf_op jit(solution)/shard_map/stage_2/pallas_call | solution.py:400
  82.6 6.8 %all-to-all-start.2 = ((f32[32,8,128]{2,1,0:T(8,128)}), f32[32,8,128]{2,1,0:T(8,128)S(1)}, u32[]{:S(2)}, u32[]{:S(2)}) async-start(f32[32,8,128]{2,1,0:T(8,128)} %bitcast.38), calls=%async_computation.2 | async-start | bytes 262144 | tf_op jit(solution)/shard_map/all_to_all | solution.py:426
  89.4 1.8 %collective-permute-start.12 = (f32[288,128]{1,0:T(8,128)}, f32[288,128]{1,0:T(8,128)S(1)}, u32[]{:S(2)}, u32[]{:S(2)}) collective-permute-start(f32[288,128]{1,0:T(8,128)} %get-tuple-element.77.refs_4_), channel_id=1, source_target_pairs={{0,4},{4,0},{8,12},{12,8},{16,20},{20,16},{24,28},{28,24},{1,5},{5... | collective-permute-start | bytes 442376 | tf_op jit(solution)/shard_map/ppermute | solution.py:421
  91.3 0.7 collective-permute-start.13
  92.0 0.9 collective-permute-start.15
  92.9 2.7 %update_2.1.refs_13_ = f32[1152,128]{1,0:T(8,128)} custom-call(f32[1152,128]{1,0:T(8,128)} %get-tuple-element.82.state, f32[1152,128]{1,0:T(8,128)} %get-tuple-element.63.refs_5_.modes, f32[256,128]{1,0:T(8,128)} %bitcast.32, f32[160,256]{1,0:T(8,128)} %get-tuple-element.76.refs_12_.inverse_rows, f32[256,128]{1,0:T(8,128)} %get-tuple-element.81.after), custom_call_target="tpu_custom_call" | custom-call | flops 150994944 | bytes 2359296 | tf_op jit(solution)/shard_map/update_2/pallas_call | solution.py:400
  95.6 3.5 %collective-permute-done.12.refs_0_ = f32[288,128]{1,0:T(8,128)S(1)} collective-permute-done((f32[288,128]{1,0:T(8,128)}, f32[288,128]{1,0:T(8,128)S(1)}, u32[]{:S(2)}, u32[]{:S(2)}) %collective-permute-start.12) | collective-permute-done | bytes 147488 | tf_op jit(solution)/shard_map/ppermute | solution.py:421
  99.1 0.6 copy-done.14
  99.9 7.5 %stage_3.1 = (f32[288,128]{1,0:T(8,128)}, f32[288,128]{1,0:T(8,128)}, f32[288,128]{1,0:T(8,128)}, f32[288,128]{1,0:T(8,128)}, f32[1152,128]{1,0:T(8,128)}, /*index=5*/f32[256,128]{1,0:T(8,128)}) custom-call(f32[1152,1152]{1,0:T(8,128)} %bitcast.25, s32[1,1152]{1,0:T(1,128)} %get-tuple-element.53.codes_row, s32[1152,128]{1,0:T(8,128)} %get-tuple-element.52.codes_lanes, ...), custom_call_target="tpu_custom_call" | custom-call | tf_op jit(solution)/shard_map/stage_3/pallas_call | solution.py:400
  107.4 6.8 %all-to-all-start.3 = ((f32[32,8,128]{2,1,0:T(8,128)}), f32[32,8,128]{2,1,0:T(8,128)S(1)}, u32[]{:S(2)}, u32[]{:S(2)}) async-start(f32[32,8,128]{2,1,0:T(8,128)} %bitcast.37), calls=%async_computation.3 | async-start | bytes 262144 | tf_op jit(solution)/shard_map/all_to_all | solution.py:426
  114.3 1.8 %collective-permute-start.16 = (f32[288,128]{1,0:T(8,128)}, f32[288,128]{1,0:T(8,128)S(1)}, u32[]{:S(2)}, u32[]{:S(2)}) collective-permute-start(f32[288,128]{1,0:T(8,128)} %get-tuple-element.83.refs_4_), channel_id=1, source_target_pairs={{0,4},{4,0},{8,12},{12,8},{16,20},{20,16},{24,28},{28,24},{1,5},{5... | collective-permute-start | bytes 442376 | tf_op jit(solution)/shard_map/ppermute | solution.py:421
  116.1 0.7 collective-permute-start.17
  116.8 0.7 collective-permute-start.19
  117.5 2.7 %update_3.1.refs_13_.step = f32[1152,128]{1,0:T(8,128)} custom-call(f32[1152,128]{1,0:T(8,128)} %get-tuple-element.88.state, f32[1152,128]{1,0:T(8,128)} %get-tuple-element.63.refs_5_.modes, f32[256,128]{1,0:T(8,128)} %bitcast.28, f32[160,256]{1,0:T(8,128)} %get-tuple-element.76.refs_12_.inverse_rows, f32[256,128]{1,0:T(8,128)} %get-tuple-element.87.after), custom_call_target="tpu_custom_call" | custom-call | flops 150994944 | bytes 2359296 | tf_op jit(solution)/shard_map/update_3/pallas_call | solution.py:400
  120.2 3.7 %collective-permute-done.16.refs_0_ = f32[288,128]{1,0:T(8,128)S(1)} collective-permute-done((f32[288,128]{1,0:T(8,128)}, f32[288,128]{1,0:T(8,128)S(1)}, u32[]{:S(2)}, u32[]{:S(2)}) %collective-permute-start.16) | collective-permute-done | bytes 147488 | tf_op jit(solution)/shard_map/ppermute | solution.py:421
  124.7 7.5 %stage_4.1 = (f32[288,128]{1,0:T(8,128)}, f32[288,128]{1,0:T(8,128)}, f32[288,128]{1,0:T(8,128)}, f32[288,128]{1,0:T(8,128)}, f32[1152,128]{1,0:T(8,128)}, /*index=5*/f32[256,128]{1,0:T(8,128)}) custom-call(f32[1152,1152]{1,0:T(8,128)} %bitcast.22, s32[1,1152]{1,0:T(1,128)} %get-tuple-element.53.codes_row, s32[1152,128]{1,0:T(8,128)} %get-tuple-element.52.codes_lanes, ...), custom_call_target="tpu_custom_call" | custom-call | tf_op jit(solution)/shard_map/stage_4/pallas_call | solution.py:400
  132.3 6.8 %all-to-all-start.4 = ((f32[32,8,128]{2,1,0:T(8,128)}), f32[32,8,128]{2,1,0:T(8,128)S(1)}, u32[]{:S(2)}, u32[]{:S(2)}) async-start(f32[32,8,128]{2,1,0:T(8,128)} %bitcast.39), calls=%async_computation.4 | async-start | bytes 262144 | tf_op jit(solution)/shard_map/all_to_all | solution.py:426
  139.1 1.8 %collective-permute-start.20 = (f32[288,128]{1,0:T(8,128)}, f32[288,128]{1,0:T(8,128)S(1)}, u32[]{:S(2)}, u32[]{:S(2)}) collective-permute-start(f32[288,128]{1,0:T(8,128)} %get-tuple-element.89.refs_4_), channel_id=1, source_target_pairs={{0,4},{4,0},{8,12},{12,8},{16,20},{20,16},{24,28},{28,24},{1,5},{5... | collective-permute-start | bytes 442376 | tf_op jit(solution)/shard_map/ppermute | solution.py:421
  140.9 0.7 collective-permute-start.21
  141.7 0.7 collective-permute-start.23
  142.4 2.7 %update_4.1.refs_13_ = f32[1152,128]{1,0:T(8,128)} custom-call(f32[1152,128]{1,0:T(8,128)} %get-tuple-element.94.state, f32[1152,128]{1,0:T(8,128)} %get-tuple-element.63.refs_5_.modes, f32[256,128]{1,0:T(8,128)} %bitcast.30, f32[160,256]{1,0:T(8,128)} %get-tuple-element.76.refs_12_.inverse_rows, f32[256,128]{1,0:T(8,128)} %get-tuple-element.93.after), custom_call_target="tpu_custom_call" | custom-call | flops 150994944 | bytes 2359296 | tf_op jit(solution)/shard_map/update_4/pallas_call | solution.py:400
  145.0 3.7 %collective-permute-done.20.refs_0_ = f32[288,128]{1,0:T(8,128)S(1)} collective-permute-done((f32[288,128]{1,0:T(8,128)}, f32[288,128]{1,0:T(8,128)S(1)}, u32[]{:S(2)}, u32[]{:S(2)}) %collective-permute-start.20) | collective-permute-done | bytes 147488 | tf_op jit(solution)/shard_map/ppermute | solution.py:421
  149.6 3.5 %stage_5.1 = (f32[1152,128]{1,0:T(8,128)}, f32[256,128]{1,0:T(8,128)}) custom-call(s32[1,1152]{1,0:T(1,128)} %get-tuple-element.53.codes_row, s32[1152,128]{1,0:T(8,128)} %get-tuple-element.52.codes_lanes, f32[288,128]{1,0:T(8,128)} %copy-done.10, f32[288,128]{1,0:T(8,128)} %copy-done.11, f32[288,128]{1,0:T(8,128)} %copy-done.12, f32[288,128]{1,0:T(8,128)} %copy-done.13, ...), custom_call_target="tpu_custom_call" | custom-call | tf_op jit(solution)/shard_map/stage_5/pallas_call | solution.py:400
  153.1 6.8 %all-to-all-start.5 = ((f32[32,8,128]{2,1,0:T(8,128)}), f32[32,8,128]{2,1,0:T(8,128)S(1)}, u32[]{:S(2)}, u32[]{:S(2)}) async-start(f32[32,8,128]{2,1,0:T(8,128)} %bitcast.43), calls=%async_computation.5 | async-start | bytes 262144 | tf_op jit(solution)/shard_map/all_to_all | solution.py:426
  160.0 6.8 %slots_to_rows.1 = (f32[1152,128]{1,0:T(8,128)}, f32[1152,128]{1,0:T(8,128)}, f32[1152,128]{1,0:T(8,128)}) custom-call(s32[1152,128]{1,0:T(8,128)} %get-tuple-element.52.codes_lanes, f32[1152,128]{1,0:T(8,128)} %get-tuple-element.95.residual, f32[1152,128]{1,0:T(8,128)} %get-tuple-element.96.raw_step, f32[1152,128]{1,0:T(8,128)} %get-tuple-element.97.start, ...), custom_call_target="tpu_custom_call" | custom-call | tf_op jit(solution)/shard_map/slots_to_rows/pallas_call | solution.py:400
  166.8 1.4 all-to-all-done.5
  168.2 0.7 copy-done.5
  168.8 2.7 %residual.1 = f32[1152,128]{1,0:T(8,128)} custom-call(f32[1152,128]{1,0:T(8,128)} %get-tuple-element.99.residual, f32[1152,128]{1,0:T(8,128)} %get-tuple-element.100.modes, f32[256,128]{1,0:T(8,128)} %bitcast.40, f32[160,256]{1,0:T(8,128)} %get-tuple-element.76.refs_12_.inverse_rows), custom_call_target="tpu_custom_call" | custom-call | tf_op jit(solution)/shard_map/residual/pallas_call | solution.py:400
  (85 shorter events, 4.4 us)
Async XLA Ops:
  3.1 22.5 %all-to-all-start = ((f32[32,8,384]{2,1,0:T(8,128)}), f32[32,8,384]{2,1,0:T(8,128)S(1)}, u32[]{:S(2)}, u32[]{:S(2)}) async-start(f32[32,8,384]{2,1,0:T(8,128)} %bitcast.41), calls=%async_computation | async-start | bytes 786432 | tf_op jit(solution)/shard_map/all_to_all | solution.py:426
  10.4 4.5 %collective-permute-start = (f32[8,288]{1,0:T(8,128)}, f32[8,288]{1,0:T(8,128)S(1)}, u32[]{:S(2)}, u32[]{:S(2)}) collective-permute-start(f32[8,288]{1,0:T(8,128)} %get-tuple-element.54.refs_0_), channel_id=1, source_target_pairs={{0,4},{4,0},{8,12},{12,8},{16,20},{20,16},{24,28},{28,24},{1,5},{5... | collective-permute-start | bytes 27656 | tf_op jit(solution)/shard_map/ppermute | solution.py:421
  12.2 2.7 %collective-permute-start.1 = (f32[8,288]{1,0:T(8,128)}, f32[8,288]{1,0:T(8,128)S(1)}, u32[]{:S(2)}, u32[]{:S(2)}) collective-permute-start(f32[8,288]{1,0:T(8,128)} %get-tuple-element.55.refs_1_), channel_id=1, source_target_pairs={{4,8},{8,4},{12,16},{16,12},{20,24},{24,20},{5,9},{9,5},{13,17},{1... | collective-permute-start | bytes 27656 | tf_op jit(solution)/shard_map/ppermute | solution.py:421
  12.8 2.1 %collective-permute-start.2 = (f32[8,288]{1,0:T(8,128)}, f32[8,288]{1,0:T(8,128)S(1)}, u32[]{:S(2)}, u32[]{:S(2)}) collective-permute-start(f32[8,288]{1,0:T(8,128)} %get-tuple-element.56.refs_2_), channel_id=1, source_target_pairs={{0,1},{1,0},{2,3},{3,2},{4,5},{5,4},{6,7},{7,6},{8,9},{9,8},{10,11... | collective-permute-start | bytes 27656 | tf_op jit(solution)/shard_map/ppermute | solution.py:421
  12.9 2.0 %collective-permute-start.3 = (f32[8,288]{1,0:T(8,128)}, f32[8,288]{1,0:T(8,128)S(1)}, u32[]{:S(2)}, u32[]{:S(2)}) collective-permute-start(f32[8,288]{1,0:T(8,128)} %get-tuple-element.57.refs_3_), channel_id=1, source_target_pairs={{1,2},{2,1},{5,6},{6,5},{9,10},{10,9},{13,14},{14,13},{17,18},{18,... | collective-permute-start | bytes 27656 | tf_op jit(solution)/shard_map/ppermute | solution.py:421
  25.6 0.7 copy-start
  33.9 9.3 %collective-permute-start.4 = (f32[432,128]{1,0:T(8,128)}, f32[432,128]{1,0:T(8,128)S(1)}, u32[]{:S(2)}, u32[]{:S(2)}) collective-permute-start(f32[432,128]{1,0:T(8,128)} %get-tuple-element.64.refs_4_), channel_id=1, source_target_pairs={{0,4},{4,0},{8,12},{12,8},{16,20},{20,16},{24,28},{28,24},{1,5},{5... | collective-permute-start | bytes 663560 | tf_op jit(solution)/shard_map/ppermute | solution.py:421
  38.4 4.8 %collective-permute-start.5 = (f32[432,128]{1,0:T(8,128)}, f32[432,128]{1,0:T(8,128)S(1)}, u32[]{:S(2)}, u32[]{:S(2)}) collective-permute-start(f32[432,128]{1,0:T(8,128)} %get-tuple-element.65.refs_5_), channel_id=1, source_target_pairs={{4,8},{8,4},{12,16},{16,12},{20,24},{24,20},{5,9},{9,5},{13,17},{1... | collective-permute-start | bytes 663560 | tf_op jit(solution)/shard_map/ppermute | solution.py:421
  39.3 4.6 %collective-permute-start.6 = (f32[432,128]{1,0:T(8,128)}, f32[432,128]{1,0:T(8,128)S(1)}, u32[]{:S(2)}, u32[]{:S(2)}) collective-permute-start(f32[432,128]{1,0:T(8,128)} %get-tuple-element.66.refs_6_), channel_id=1, source_target_pairs={{0,1},{1,0},{2,3},{3,2},{4,5},{5,4},{6,7},{7,6},{8,9},{9,8},{10,11... | collective-permute-start | bytes 663560 | tf_op jit(solution)/shard_map/ppermute | solution.py:421
  42.5 1.3 collective-permute-start.7
  43.2 0.8 copy-start.7
  43.8 0.8 copy-start.9
  51.5 22.9 %all-to-all-start.1 = ((f32[32,8,128]{2,1,0:T(8,128)}), f32[32,8,128]{2,1,0:T(8,128)S(1)}, u32[]{:S(2)}, u32[]{:S(2)}) async-start(f32[32,8,128]{2,1,0:T(8,128)} %bitcast.42), calls=%async_computation.1 | async-start | bytes 262144 | tf_op jit(solution)/shard_map/all_to_all | solution.py:426
  64.8 9.6 %collective-permute-start.8 = (f32[288,128]{1,0:T(8,128)}, f32[288,128]{1,0:T(8,128)S(1)}, u32[]{:S(2)}, u32[]{:S(2)}) collective-permute-start(f32[288,128]{1,0:T(8,128)} %get-tuple-element.69.refs_4_), channel_id=1, source_target_pairs={{0,4},{4,0},{8,12},{12,8},{16,20},{20,16},{24,28},{28,24},{1,5},{5... | collective-permute-start | bytes 442376 | tf_op jit(solution)/shard_map/ppermute | solution.py:421
  66.6 7.8 %collective-permute-start.9 = (f32[288,128]{1,0:T(8,128)}, f32[288,128]{1,0:T(8,128)S(1)}, u32[]{:S(2)}, u32[]{:S(2)}) collective-permute-start(f32[288,128]{1,0:T(8,128)} %get-tuple-element.70.refs_5_), channel_id=1, source_target_pairs={{4,8},{8,4},{12,16},{16,12},{20,24},{24,20},{5,9},{9,5},{13,17},{1... | collective-permute-start | bytes 442376 | tf_op jit(solution)/shard_map/ppermute | solution.py:421
  67.3 7.1 %collective-permute-start.10 = (f32[288,128]{1,0:T(8,128)}, f32[288,128]{1,0:T(8,128)S(1)}, u32[]{:S(2)}, u32[]{:S(2)}) collective-permute-start(f32[288,128]{1,0:T(8,128)} %get-tuple-element.71.refs_6_), channel_id=1, source_target_pairs={{0,1},{1,0},{2,3},{3,2},{4,5},{5,4},{6,7},{7,6},{8,9},{9,8},{10,11... | collective-permute-start | bytes 442376 | tf_op jit(solution)/shard_map/ppermute | solution.py:421
  67.4 7.1 %collective-permute-start.11 = (f32[288,128]{1,0:T(8,128)}, f32[288,128]{1,0:T(8,128)S(1)}, u32[]{:S(2)}, u32[]{:S(2)}) collective-permute-start(f32[288,128]{1,0:T(8,128)} %get-tuple-element.72.refs_7_), channel_id=1, source_target_pairs={{1,2},{2,1},{5,6},{6,5},{9,10},{10,9},{13,14},{14,13},{17,18},{18,... | collective-permute-start | bytes 442376 | tf_op jit(solution)/shard_map/ppermute | solution.py:421
  74.4 0.8 copy-start.24
  74.4 0.8 copy-start.25
  74.4 0.8 copy-start.3
  82.6 16.5 %all-to-all-start.2 = ((f32[32,8,128]{2,1,0:T(8,128)}), f32[32,8,128]{2,1,0:T(8,128)S(1)}, u32[]{:S(2)}, u32[]{:S(2)}) async-start(f32[32,8,128]{2,1,0:T(8,128)} %bitcast.38), calls=%async_computation.2 | async-start | bytes 262144 | tf_op jit(solution)/shard_map/all_to_all | solution.py:426
  89.4 9.6 %collective-permute-start.12 = (f32[288,128]{1,0:T(8,128)}, f32[288,128]{1,0:T(8,128)S(1)}, u32[]{:S(2)}, u32[]{:S(2)}) collective-permute-start(f32[288,128]{1,0:T(8,128)} %get-tuple-element.77.refs_4_), channel_id=1, source_target_pairs={{0,4},{4,0},{8,12},{12,8},{16,20},{20,16},{24,28},{28,24},{1,5},{5... | collective-permute-start | bytes 442376 | tf_op jit(solution)/shard_map/ppermute | solution.py:421
  91.3 7.8 %collective-permute-start.13 = (f32[288,128]{1,0:T(8,128)}, f32[288,128]{1,0:T(8,128)S(1)}, u32[]{:S(2)}, u32[]{:S(2)}) collective-permute-start(f32[288,128]{1,0:T(8,128)} %get-tuple-element.78.refs_5_), channel_id=1, source_target_pairs={{4,8},{8,4},{12,16},{16,12},{20,24},{24,20},{5,9},{9,5},{13,17},{1... | collective-permute-start | bytes 442376 | tf_op jit(solution)/shard_map/ppermute | solution.py:421
  91.9 7.1 %collective-permute-start.14 = (f32[288,128]{1,0:T(8,128)}, f32[288,128]{1,0:T(8,128)S(1)}, u32[]{:S(2)}, u32[]{:S(2)}) collective-permute-start(f32[288,128]{1,0:T(8,128)} %get-tuple-element.79.refs_6_), channel_id=1, source_target_pairs={{0,1},{1,0},{2,3},{3,2},{4,5},{5,4},{6,7},{7,6},{8,9},{9,8},{10,11... | collective-permute-start | bytes 442376 | tf_op jit(solution)/shard_map/ppermute | solution.py:421
  92.0 7.1 %collective-permute-start.15 = (f32[288,128]{1,0:T(8,128)}, f32[288,128]{1,0:T(8,128)S(1)}, u32[]{:S(2)}, u32[]{:S(2)}) collective-permute-start(f32[288,128]{1,0:T(8,128)} %get-tuple-element.80.refs_7_), channel_id=1, source_target_pairs={{1,2},{2,1},{5,6},{6,5},{9,10},{10,9},{13,14},{14,13},{17,18},{18,... | collective-permute-start | bytes 442376 | tf_op jit(solution)/shard_map/ppermute | solution.py:421
  99.0 0.7 copy-start.16
  99.1 0.8 copy-start.19
  99.1 0.8 copy-start.22
  99.1 0.8 copy-start.1
  107.4 16.5 %all-to-all-start.3 = ((f32[32,8,128]{2,1,0:T(8,128)}), f32[32,8,128]{2,1,0:T(8,128)S(1)}, u32[]{:S(2)}, u32[]{:S(2)}) async-start(f32[32,8,128]{2,1,0:T(8,128)} %bitcast.37), calls=%async_computation.3 | async-start | bytes 262144 | tf_op jit(solution)/shard_map/all_to_all | solution.py:426
  114.3 9.6 %collective-permute-start.16 = (f32[288,128]{1,0:T(8,128)}, f32[288,128]{1,0:T(8,128)S(1)}, u32[]{:S(2)}, u32[]{:S(2)}) collective-permute-start(f32[288,128]{1,0:T(8,128)} %get-tuple-element.83.refs_4_), channel_id=1, source_target_pairs={{0,4},{4,0},{8,12},{12,8},{16,20},{20,16},{24,28},{28,24},{1,5},{5... | collective-permute-start | bytes 442376 | tf_op jit(solution)/shard_map/ppermute | solution.py:421
  116.1 7.8 %collective-permute-start.17 = (f32[288,128]{1,0:T(8,128)}, f32[288,128]{1,0:T(8,128)S(1)}, u32[]{:S(2)}, u32[]{:S(2)}) collective-permute-start(f32[288,128]{1,0:T(8,128)} %get-tuple-element.84.refs_5_), channel_id=1, source_target_pairs={{4,8},{8,4},{12,16},{16,12},{20,24},{24,20},{5,9},{9,5},{13,17},{1... | collective-permute-start | bytes 442376 | tf_op jit(solution)/shard_map/ppermute | solution.py:421
  116.7 7.1 %collective-permute-start.18 = (f32[288,128]{1,0:T(8,128)}, f32[288,128]{1,0:T(8,128)S(1)}, u32[]{:S(2)}, u32[]{:S(2)}) collective-permute-start(f32[288,128]{1,0:T(8,128)} %get-tuple-element.85.refs_6_), channel_id=1, source_target_pairs={{0,1},{1,0},{2,3},{3,2},{4,5},{5,4},{6,7},{7,6},{8,9},{9,8},{10,11... | collective-permute-start | bytes 442376 | tf_op jit(solution)/shard_map/ppermute | solution.py:421
  116.8 7.1 %collective-permute-start.19 = (f32[288,128]{1,0:T(8,128)}, f32[288,128]{1,0:T(8,128)S(1)}, u32[]{:S(2)}, u32[]{:S(2)}) collective-permute-start(f32[288,128]{1,0:T(8,128)} %get-tuple-element.86.refs_7_), channel_id=1, source_target_pairs={{1,2},{2,1},{5,6},{6,5},{9,10},{10,9},{13,14},{14,13},{17,18},{18,... | collective-permute-start | bytes 442376 | tf_op jit(solution)/shard_map/ppermute | solution.py:421
  123.9 0.7 copy-start.17
  123.9 0.7 copy-start.20
  123.9 0.8 copy-start.23
  123.9 0.8 copy-start.2
  132.3 16.5 %all-to-all-start.4 = ((f32[32,8,128]{2,1,0:T(8,128)}), f32[32,8,128]{2,1,0:T(8,128)S(1)}, u32[]{:S(2)}, u32[]{:S(2)}) async-start(f32[32,8,128]{2,1,0:T(8,128)} %bitcast.39), calls=%async_computation.4 | async-start | bytes 262144 | tf_op jit(solution)/shard_map/all_to_all | solution.py:426
  139.1 9.6 %collective-permute-start.20 = (f32[288,128]{1,0:T(8,128)}, f32[288,128]{1,0:T(8,128)S(1)}, u32[]{:S(2)}, u32[]{:S(2)}) collective-permute-start(f32[288,128]{1,0:T(8,128)} %get-tuple-element.89.refs_4_), channel_id=1, source_target_pairs={{0,4},{4,0},{8,12},{12,8},{16,20},{20,16},{24,28},{28,24},{1,5},{5... | collective-permute-start | bytes 442376 | tf_op jit(solution)/shard_map/ppermute | solution.py:421
  140.9 7.8 %collective-permute-start.21 = (f32[288,128]{1,0:T(8,128)}, f32[288,128]{1,0:T(8,128)S(1)}, u32[]{:S(2)}, u32[]{:S(2)}) collective-permute-start(f32[288,128]{1,0:T(8,128)} %get-tuple-element.90.refs_5_), channel_id=1, source_target_pairs={{4,8},{8,4},{12,16},{16,12},{20,24},{24,20},{5,9},{9,5},{13,17},{1... | collective-permute-start | bytes 442376 | tf_op jit(solution)/shard_map/ppermute | solution.py:421
  141.6 7.1 %collective-permute-start.22 = (f32[288,128]{1,0:T(8,128)}, f32[288,128]{1,0:T(8,128)S(1)}, u32[]{:S(2)}, u32[]{:S(2)}) collective-permute-start(f32[288,128]{1,0:T(8,128)} %get-tuple-element.91.refs_6_), channel_id=1, source_target_pairs={{0,1},{1,0},{2,3},{3,2},{4,5},{5,4},{6,7},{7,6},{8,9},{9,8},{10,11... | collective-permute-start | bytes 442376 | tf_op jit(solution)/shard_map/ppermute | solution.py:421
  141.7 7.1 %collective-permute-start.23 = (f32[288,128]{1,0:T(8,128)}, f32[288,128]{1,0:T(8,128)S(1)}, u32[]{:S(2)}, u32[]{:S(2)}) collective-permute-start(f32[288,128]{1,0:T(8,128)} %get-tuple-element.92.refs_7_), channel_id=1, source_target_pairs={{1,2},{2,1},{5,6},{6,5},{9,10},{10,9},{13,14},{14,13},{17,18},{18,... | collective-permute-start | bytes 442376 | tf_op jit(solution)/shard_map/ppermute | solution.py:421
  148.7 0.7 copy-start.11
  148.7 0.7 copy-start.12
  148.8 0.8 copy-start.13
  148.8 0.8 copy-start.4
  153.1 15.1 %all-to-all-start.5 = ((f32[32,8,128]{2,1,0:T(8,128)}), f32[32,8,128]{2,1,0:T(8,128)S(1)}, u32[]{:S(2)}, u32[]{:S(2)}) async-start(f32[32,8,128]{2,1,0:T(8,128)} %bitcast.43), calls=%async_computation.5 | async-start | bytes 262144 | tf_op jit(solution)/shard_map/all_to_all | solution.py:426
  (12 other events, 7.8 us)
